TPU v7x, 256 devices: a whole 4x4x8 slice. The times are simulated.
256 devices in a mesh: wide: 64 (over x_lo, y, z), narrow: 4 (over x_hi, core).
Axes of the slice: x: 4 (x_hi: 2, x_lo: 2; x = x_hi * 2 + x_lo), y: 4, z: 8, core: 2. Of those that a mesh axis runs over, the one named last changes fastest.
Arguments:
- patches_in: bfloat16 [512, 64, 768], P('wide'), may hold values from -6 to 6
- w_up: bfloat16 [768, 3072], P(None, 'narrow'), may hold values from -0.21875 to 0.21875
- w_down: bfloat16 [3072, 768], P('narrow'), may hold values from -0.109375 to 0.109375
- captions: bfloat16 [512, 32, 768], P(('wide', 'narrow')), may hold values from -11 to 11
- labels: int32 [512], P(('wide', 'narrow')), may hold values from 0 to 511, each once
- lengths: int32 [512], P(('wide', 'narrow')), may hold values from 4 to 32
Outputs:
- grad_images: float32 [512, 64, 768], P(('wide', 'narrow'))
- grad_captions: float32 [512, 32, 768], P(('wide', 'narrow'))
Inputs may be any that keep to these rules, and one draw needn't show every extreme that they name: `labels`: each image is named by exactly one caption.
All inputs are finite; a program needn't handle non-finite values.
Results may differ from a plain program's by a relative error of at most 0.019.
Values may be sent and summed in bfloat16 or wider, within the bound.
A program may use at most 192 MiB of HBM per device.

v0:
```python
import math

import jax
import jax.numpy as jnp
from jax import lax
from jax.sharding import PartitionSpec as P

SCORE_GAIN = 1.75
LOGIT_SCALE = 4.0
LOGIT_BIAS = -26.0
NORM_EPS = 1e-06
MASKED = -1e30


def from_behind(array, axis, by):
    length = lax.axis_size(axis)
    return lax.ppermute(array, axis, [(i, (i + by) % length) for i in range(length)])


def layer_norm(mixed):
    center = mixed - jnp.mean(mixed, axis=-1, keepdims=True)
    spread = jnp.mean(center * center, axis=-1, keepdims=True)
    return center * lax.rsqrt(spread + NORM_EPS)


def pair_terms(images, caption_part, label_part, length_part, image_base, num_patch):
    part_caps, num_tok, feature_dim = caption_part.shape
    num_rows = images.shape[0]
    num_images = num_rows // num_patch
    factor = SCORE_GAIN / math.sqrt(feature_dim)
    flat_text = caption_part.reshape(part_caps * num_tok, feature_dim)
    scores = (
        lax.dot_general(
            flat_text, images, (((1,), (1,)), ((), ())), preferred_element_type=jnp.float32
        )
        * factor
    )
    scores = scores.reshape(part_caps, num_tok, num_images, num_patch)
    valid = (jnp.arange(num_tok, dtype=jnp.int32)[None, :] < length_part[:, None]).astype(
        jnp.float32
    )
    masked_scores = jnp.where(valid[:, :, None, None] > 0.5, scores, MASKED)
    patch_top = jnp.max(masked_scores, axis=1, keepdims=True)
    patch_exp = jnp.exp(masked_scores - patch_top)
    patch_total = jnp.sum(patch_exp, axis=1, keepdims=True)
    patch_pool = (patch_top + jnp.log(patch_total))[:, 0]
    patch_weight = patch_exp / patch_total
    token_top = jnp.max(scores, axis=3, keepdims=True)
    token_exp = jnp.exp(scores - token_top)
    token_total = jnp.sum(token_exp, axis=3, keepdims=True)
    token_pool = (token_top + jnp.log(token_total))[..., 0]
    token_weight = token_exp / token_total
    length_float = length_part.astype(jnp.float32)
    similarity = 0.5 * (
        jnp.mean(patch_pool, axis=2)
        + jnp.sum(valid[:, :, None] * token_pool, axis=1) / length_float[:, None]
    )
    logit = LOGIT_SCALE * similarity + LOGIT_BIAS
    image_ids = image_base + jnp.arange(num_images, dtype=jnp.int32)
    sign = jnp.where(label_part[:, None] == image_ids[None, :], 1.0, -1.0).astype(jnp.float32)
    pair_grad = -sign * jax.nn.sigmoid(-sign * logit)
    token_share = valid / length_float[:, None]
    score_grad = (
        0.5
        * LOGIT_SCALE
        * factor
        * pair_grad[:, None, :, None]
        * (patch_weight / num_patch + token_share[:, :, None, None] * token_weight)
    )
    score_grad = score_grad.reshape(part_caps * num_tok, num_rows).astype(jnp.bfloat16)
    text_grad = jnp.dot(score_grad, images, preferred_element_type=jnp.float32).reshape(
        part_caps, num_tok, feature_dim
    )
    return (score_grad, text_grad)


def shards(patches_in, w_up, w_down, captions, labels, lengths):
    num_group, num_patch, feature_dim = patches_in.shape
    num_rows = num_group * num_patch
    own_caps = captions.shape[0]
    num_tok = captions.shape[1]
    text_rows = own_caps * num_tok
    narrow_size = lax.axis_size("narrow")
    wide_size = lax.axis_size("wide")
    wide_index = lax.axis_index("wide")
    flat_in = patches_in.reshape(num_rows, feature_dim)
    hidden = jax.nn.gelu(jnp.dot(flat_in, w_up, preferred_element_type=jnp.float32)).astype(
        jnp.bfloat16
    )
    summed_out = lax.psum(jnp.dot(hidden, w_down, preferred_element_type=jnp.float32), "narrow")
    images = layer_norm(flat_in.astype(jnp.float32) + summed_out).astype(jnp.bfloat16)
    cycle_labels, cycle_lengths = (
        lax.all_gather(labels, "wide", axis=0, tiled=True),
        lax.all_gather(lengths, "wide", axis=0, tiled=True),
    )
    image_base = wide_index * num_group

    def shift_turn(turn_index, state_now):
        moving_text, moving_grad, text_store, grad_store = state_now
        anchor = (wide_index - turn_index) % wide_size
        label_part = lax.dynamic_slice_in_dim(cycle_labels, anchor * own_caps, own_caps, 0)
        length_part = lax.dynamic_slice_in_dim(cycle_lengths, anchor * own_caps, own_caps, 0)
        score_grad, text_grad = pair_terms(
            images, moving_text, label_part, length_part, image_base, num_patch
        )
        text_store = lax.dynamic_update_slice_in_dim(
            text_store, moving_text.reshape(1, text_rows, feature_dim), turn_index, 0
        )
        grad_store = lax.dynamic_update_slice_in_dim(
            grad_store, score_grad.reshape(1, text_rows, num_rows), turn_index, 0
        )
        moving_grad = from_behind(moving_grad + text_grad, "wide", 1)
        moving_text = from_behind(moving_text, "wide", 1)
        return (moving_text, moving_grad, text_store, grad_store)

    start_state = (
        captions,
        jnp.zeros(captions.shape, jnp.float32),
        jnp.zeros((wide_size, text_rows, feature_dim), jnp.bfloat16),
        jnp.zeros((wide_size, text_rows, num_rows), jnp.bfloat16),
    )
    final_state = lax.fori_loop(0, wide_size, shift_turn, start_state)
    caption_grad = final_state[1]
    image_grad = lax.dot_general(
        final_state[3].reshape(wide_size * text_rows, num_rows),
        final_state[2].reshape(wide_size * text_rows, feature_dim),
        (((0,), (0,)), ((), ())),
        preferred_element_type=jnp.float32,
    )
    image_share = lax.psum_scatter(
        image_grad.astype(jnp.bfloat16), "narrow", scatter_dimension=0, tiled=True
    ).astype(jnp.float32)
    return (image_share.reshape(num_group // narrow_size, num_patch, feature_dim), caption_grad)


def solution(mesh):
    return jax.shard_map(
        shards,
        mesh=mesh,
        in_specs=(
            P("wide", None, None),
            P(None, "narrow"),
            P("narrow", None),
            P(("wide", "narrow"), None, None),
            P(("wide", "narrow")),
            P(("wide", "narrow")),
        ),
        out_specs=(P(("wide", "narrow"), None, None), P(("wide", "narrow"), None, None)),
        check_vma=False,
    )
```

profile of v0, /device:TPU:1, one launch (start us, length us, event | category | flops | bytes accessed | tf_op | source)
XLA Modules:
  0.0 1113.5 jit_solution(5766300679633398448)
XLA Ops:
  15.1 23.1 %all-reduce.2 = (s32[128]{0:T(128)S(1)}, s32[128]{0:T(128)S(1)}) all-reduce(s32[128]{0:T(128)S(1)} %dynamic-update-slice, s32[128]{0:T(128)S(1)} %dynamic-update-slice.1), channel_id=1, replica_groups=mesh['wide'=64,'narrow'=4] {'wide'}, use_global_device_ids=true, to_apply=%add | all-reduce | flops 256 | bytes 2048
  38.1 35.3 %all-reduce.5.cloned.1.call-done = f32[512,768]{1,0:T(8,128)} async-done(((f32[512,768]{1,0:T(8,128)}), f32[512,768]{1,0:T(8,128)}) %all-reduce.5.cloned.1.call-update) | async-done | bytes 1572880 | tf_op jit(solution)/shard_map/psum | solution.py:90
  76.7 922.8 %while.21 = (s32[]{:T(128)}, bf16[2,32,768]{2,1,0:T(8,128)(2,1)S(1)}, f32[2,32,768]{2,1,0:T(8,128)S(1)}, bf16[64,64,768]{2,1,0:T(8,128)(2,1)}, bf16[64,64,512]{2...) while((s32[]{:T(128)}, ...), condition=%wide.region_10.11_spmd, body=%wide.region_3.10_spmd.sunk | while | flops 101336136 | bytes 7287608 | solution.py:122
  97.7 10.9 collective-permute-done
  251.5 11.1 collective-permute-done
  267.2 12.5 %collective-permute-done = bf16[2,32,768]{2,1,0:T(8,128)(2,1)S(1)} collective-permute-done((bf16[2,32,768]{2,1,0:T(8,128)(2,1)S(1)}, bf16[2,32,768]{2,1,0:T(8,128)(2,1)S(1)}, u32[]{:S(2)}, u32[]{:S(2)}) %collective-permute-start) | collective-permute-done | bytes 98336 | tf_op jit(solution)/shard_map/while/body/eval_jaxpr/ppermute | solution.py:17
  284.3 11.7 %collective-permute-done = bf16[2,32,768]{2,1,0:T(8,128)(2,1)S(1)} collective-permute-done((bf16[2,32,768]{2,1,0:T(8,128)(2,1)S(1)}, bf16[2,32,768]{2,1,0:T(8,128)(2,1)S(1)}, u32[]{:S(2)}, u32[]{:S(2)}) %collective-permute-start) | collective-permute-done | bytes 98336 | tf_op jit(solution)/shard_map/while/body/eval_jaxpr/ppermute | solution.py:17
  300.5 10.7 collective-permute-done
  439.5 10.1 collective-permute-done
  454.2 11.2 %collective-permute-done = bf16[2,32,768]{2,1,0:T(8,128)(2,1)S(1)} collective-permute-done((bf16[2,32,768]{2,1,0:T(8,128)(2,1)S(1)}, bf16[2,32,768]{2,1,0:T(8,128)(2,1)S(1)}, u32[]{:S(2)}, u32[]{:S(2)}) %collective-permute-start) | collective-permute-done | bytes 98336 | tf_op jit(solution)/shard_map/while/body/eval_jaxpr/ppermute | solution.py:17
  470.0 12.3 %collective-permute-done = bf16[2,32,768]{2,1,0:T(8,128)(2,1)S(1)} collective-permute-done((bf16[2,32,768]{2,1,0:T(8,128)(2,1)S(1)}, bf16[2,32,768]{2,1,0:T(8,128)(2,1)S(1)}, u32[]{:S(2)}, u32[]{:S(2)}) %collective-permute-start) | collective-permute-done | bytes 98336 | tf_op jit(solution)/shard_map/while/body/eval_jaxpr/ppermute | solution.py:17
  487.0 11.5 %collective-permute-done = bf16[2,32,768]{2,1,0:T(8,128)(2,1)S(1)} collective-permute-done((bf16[2,32,768]{2,1,0:T(8,128)(2,1)S(1)}, bf16[2,32,768]{2,1,0:T(8,128)(2,1)S(1)}, u32[]{:S(2)}, u32[]{:S(2)}) %collective-permute-start) | collective-permute-done | bytes 98336 | tf_op jit(solution)/shard_map/while/body/eval_jaxpr/ppermute | solution.py:17
  503.1 10.6 collective-permute-done
  641.8 10.3 collective-permute-done
  656.7 11.3 %collective-permute-done = bf16[2,32,768]{2,1,0:T(8,128)(2,1)S(1)} collective-permute-done((bf16[2,32,768]{2,1,0:T(8,128)(2,1)S(1)}, bf16[2,32,768]{2,1,0:T(8,128)(2,1)S(1)}, u32[]{:S(2)}, u32[]{:S(2)}) %collective-permute-start) | collective-permute-done | bytes 98336 | tf_op jit(solution)/shard_map/while/body/eval_jaxpr/ppermute | solution.py:17
  672.6 12.2 %collective-permute-done = bf16[2,32,768]{2,1,0:T(8,128)(2,1)S(1)} collective-permute-done((bf16[2,32,768]{2,1,0:T(8,128)(2,1)S(1)}, bf16[2,32,768]{2,1,0:T(8,128)(2,1)S(1)}, u32[]{:S(2)}, u32[]{:S(2)}) %collective-permute-start) | collective-permute-done | bytes 98336 | tf_op jit(solution)/shard_map/while/body/eval_jaxpr/ppermute | solution.py:17
  689.4 11.3 %collective-permute-done = bf16[2,32,768]{2,1,0:T(8,128)(2,1)S(1)} collective-permute-done((bf16[2,32,768]{2,1,0:T(8,128)(2,1)S(1)}, bf16[2,32,768]{2,1,0:T(8,128)(2,1)S(1)}, u32[]{:S(2)}, u32[]{:S(2)}) %collective-permute-start) | collective-permute-done | bytes 98336 | tf_op jit(solution)/shard_map/while/body/eval_jaxpr/ppermute | solution.py:17
  705.3 10.4 collective-permute-done
  843.8 10.4 collective-permute-done
  858.9 11.5 %collective-permute-done = bf16[2,32,768]{2,1,0:T(8,128)(2,1)S(1)} collective-permute-done((bf16[2,32,768]{2,1,0:T(8,128)(2,1)S(1)}, bf16[2,32,768]{2,1,0:T(8,128)(2,1)S(1)}, u32[]{:S(2)}, u32[]{:S(2)}) %collective-permute-start) | collective-permute-done | bytes 98336 | tf_op jit(solution)/shard_map/while/body/eval_jaxpr/ppermute | solution.py:17
  875.0 12.1 %collective-permute-done = bf16[2,32,768]{2,1,0:T(8,128)(2,1)S(1)} collective-permute-done((bf16[2,32,768]{2,1,0:T(8,128)(2,1)S(1)}, bf16[2,32,768]{2,1,0:T(8,128)(2,1)S(1)}, u32[]{:S(2)}, u32[]{:S(2)}) %collective-permute-start) | collective-permute-done | bytes 98336 | tf_op jit(solution)/shard_map/while/body/eval_jaxpr/ppermute | solution.py:17
  891.7 11.1 collective-permute-done
  907.4 10.2 collective-permute-done
  1007.9 96.3 %reduce-scatter.2.cloned.1.call-done = bf16[128,768]{1,0:T(8,128)(2,1)} async-done(((bf16[512,768]{1,0:T(8,128)(2,1)}), bf16[128,768]{1,0:T(8,128)(2,1)}) %reduce-scatter.2.cloned.1.call-update) | async-done | bytes 196624 | tf_op jit(solution)/shard_map/reduce_scatter | solution.py:130
  (2063 shorter events, 715.1 us)
Async XLA Ops:
  7.2 66.3 %all-reduce.5.cloned.1.call-start = ((), (), s32[]{:S(2)}) async-start(), calls=%async_computation.1 | async-start | bytes 3145728 | tf_op jit(solution)/shard_map/psum | solution.py:90
  12.8 1091.5 %reduce-scatter.2.cloned.1.call-start = ((), (), s32[]{:S(2)}) async-start(), calls=%async_computation.2 | async-start | bytes 983040 | tf_op jit(solution)/shard_map/reduce_scatter | solution.py:130
  80.4 12.6 %collective-permute-start.1 = (f32[2,32,768]{2,1,0:T(8,128)S(1)}, f32[2,32,768]{2,1,0:T(8,128)S(1)}, u32[]{:S(2)}, u32[]{:S(2)}) collective-permute-start(f32[2,32,768]{2,1,0:T(8,128)S(1)} %convolution_add_fusion.2), channel_id=1, source_target_pairs={{0,4},{4,8},{8,12},{12,16},{16,20},{20,24},{24,28},{28,32},{32,36}... | collective-permute-start | bytes 589832 | tf_op jit(solution)/shard_map/while/body/eval_jaxpr/ppermute | solution.py:17
  266.4 13.3 %collective-permute-start.1 = (f32[2,32,768]{2,1,0:T(8,128)S(1)}, f32[2,32,768]{2,1,0:T(8,128)S(1)}, u32[]{:S(2)}, u32[]{:S(2)}) collective-permute-start(f32[2,32,768]{2,1,0:T(8,128)S(1)} %convolution_add_fusion.2), channel_id=1, source_target_pairs={{0,4},{4,8},{8,12},{12,16},{16,20},{20,24},{24,28},{28,32},{32,36}... | collective-permute-start | bytes 589832 | tf_op jit(solution)/shard_map/while/body/eval_jaxpr/ppermute | solution.py:17
  266.4 13.2 %collective-permute-start = (bf16[2,32,768]{2,1,0:T(8,128)(2,1)S(1)}, bf16[2,32,768]{2,1,0:T(8,128)(2,1)S(1)}, u32[]{:S(2)}, u32[]{:S(2)}) collective-permute-start(bf16[2,32,768]{2,1,0:T(8,128)(2,1)S(1)} %copy.19), channel_id=1, source_target_pairs={{0,4},{4,8},{8,12},{12,16},{16,20},{20,24},{24,28},{28,32},{32,36}... | collective-permute-start | bytes 294920 | tf_op jit(solution)/shard_map/while/body/eval_jaxpr/ppermute | solution.py:17
  283.4 12.5 %collective-permute-start.1 = (f32[2,32,768]{2,1,0:T(8,128)S(1)}, f32[2,32,768]{2,1,0:T(8,128)S(1)}, u32[]{:S(2)}, u32[]{:S(2)}) collective-permute-start(f32[2,32,768]{2,1,0:T(8,128)S(1)} %convolution_add_fusion.2), channel_id=1, source_target_pairs={{0,4},{4,8},{8,12},{12,16},{16,20},{20,24},{24,28},{28,32},{32,36}... | collective-permute-start | bytes 589832 | tf_op jit(solution)/shard_map/while/body/eval_jaxpr/ppermute | solution.py:17
  283.5 12.4 %collective-permute-start = (bf16[2,32,768]{2,1,0:T(8,128)(2,1)S(1)}, bf16[2,32,768]{2,1,0:T(8,128)(2,1)S(1)}, u32[]{:S(2)}, u32[]{:S(2)}) collective-permute-start(bf16[2,32,768]{2,1,0:T(8,128)(2,1)S(1)} %copy.19), channel_id=1, source_target_pairs={{0,4},{4,8},{8,12},{12,16},{16,20},{20,24},{24,28},{28,32},{32,36}... | collective-permute-start | bytes 294920 | tf_op jit(solution)/shard_map/while/body/eval_jaxpr/ppermute | solution.py:17
  453.4 12.1 %collective-permute-start.1 = (f32[2,32,768]{2,1,0:T(8,128)S(1)}, f32[2,32,768]{2,1,0:T(8,128)S(1)}, u32[]{:S(2)}, u32[]{:S(2)}) collective-permute-start(f32[2,32,768]{2,1,0:T(8,128)S(1)} %convolution_add_fusion.2), channel_id=1, source_target_pairs={{0,4},{4,8},{8,12},{12,16},{16,20},{20,24},{24,28},{28,32},{32,36}... | collective-permute-start | bytes 589832 | tf_op jit(solution)/shard_map/while/body/eval_jaxpr/ppermute | solution.py:17
  453.5 12.0 %collective-permute-start = (bf16[2,32,768]{2,1,0:T(8,128)(2,1)S(1)}, bf16[2,32,768]{2,1,0:T(8,128)(2,1)S(1)}, u32[]{:S(2)}, u32[]{:S(2)}) collective-permute-start(bf16[2,32,768]{2,1,0:T(8,128)(2,1)S(1)} %copy.19), channel_id=1, source_target_pairs={{0,4},{4,8},{8,12},{12,16},{16,20},{20,24},{24,28},{28,32},{32,36}... | collective-permute-start | bytes 294920 | tf_op jit(solution)/shard_map/while/body/eval_jaxpr/ppermute | solution.py:17
  469.2 13.1 %collective-permute-start.1 = (f32[2,32,768]{2,1,0:T(8,128)S(1)}, f32[2,32,768]{2,1,0:T(8,128)S(1)}, u32[]{:S(2)}, u32[]{:S(2)}) collective-permute-start(f32[2,32,768]{2,1,0:T(8,128)S(1)} %convolution_add_fusion.2), channel_id=1, source_target_pairs={{0,4},{4,8},{8,12},{12,16},{16,20},{20,24},{24,28},{28,32},{32,36}... | collective-permute-start | bytes 589832 | tf_op jit(solution)/shard_map/while/body/eval_jaxpr/ppermute | solution.py:17
  469.3 13.1 %collective-permute-start = (bf16[2,32,768]{2,1,0:T(8,128)(2,1)S(1)}, bf16[2,32,768]{2,1,0:T(8,128)(2,1)S(1)}, u32[]{:S(2)}, u32[]{:S(2)}) collective-permute-start(bf16[2,32,768]{2,1,0:T(8,128)(2,1)S(1)} %copy.19), channel_id=1, source_target_pairs={{0,4},{4,8},{8,12},{12,16},{16,20},{20,24},{24,28},{28,32},{32,36}... | collective-permute-start | bytes 294920 | tf_op jit(solution)/shard_map/while/body/eval_jaxpr/ppermute | solution.py:17
  486.2 12.3 %collective-permute-start.1 = (f32[2,32,768]{2,1,0:T(8,128)S(1)}, f32[2,32,768]{2,1,0:T(8,128)S(1)}, u32[]{:S(2)}, u32[]{:S(2)}) collective-permute-start(f32[2,32,768]{2,1,0:T(8,128)S(1)} %convolution_add_fusion.2), channel_id=1, source_target_pairs={{0,4},{4,8},{8,12},{12,16},{16,20},{20,24},{24,28},{28,32},{32,36}... | collective-permute-start | bytes 589832 | tf_op jit(solution)/shard_map/while/body/eval_jaxpr/ppermute | solution.py:17
  486.2 12.2 %collective-permute-start = (bf16[2,32,768]{2,1,0:T(8,128)(2,1)S(1)}, bf16[2,32,768]{2,1,0:T(8,128)(2,1)S(1)}, u32[]{:S(2)}, u32[]{:S(2)}) collective-permute-start(bf16[2,32,768]{2,1,0:T(8,128)(2,1)S(1)} %copy.19), channel_id=1, source_target_pairs={{0,4},{4,8},{8,12},{12,16},{16,20},{20,24},{24,28},{28,32},{32,36}... | collective-permute-start | bytes 294920 | tf_op jit(solution)/shard_map/while/body/eval_jaxpr/ppermute | solution.py:17
  655.8 12.2 %collective-permute-start.1 = (f32[2,32,768]{2,1,0:T(8,128)S(1)}, f32[2,32,768]{2,1,0:T(8,128)S(1)}, u32[]{:S(2)}, u32[]{:S(2)}) collective-permute-start(f32[2,32,768]{2,1,0:T(8,128)S(1)} %convolution_add_fusion.2), channel_id=1, source_target_pairs={{0,4},{4,8},{8,12},{12,16},{16,20},{20,24},{24,28},{28,32},{32,36}... | collective-permute-start | bytes 589832 | tf_op jit(solution)/shard_map/while/body/eval_jaxpr/ppermute | solution.py:17
  655.9 12.1 %collective-permute-start = (bf16[2,32,768]{2,1,0:T(8,128)(2,1)S(1)}, bf16[2,32,768]{2,1,0:T(8,128)(2,1)S(1)}, u32[]{:S(2)}, u32[]{:S(2)}) collective-permute-start(bf16[2,32,768]{2,1,0:T(8,128)(2,1)S(1)} %copy.19), channel_id=1, source_target_pairs={{0,4},{4,8},{8,12},{12,16},{16,20},{20,24},{24,28},{28,32},{32,36}... | collective-permute-start | bytes 294920 | tf_op jit(solution)/shard_map/while/body/eval_jaxpr/ppermute | solution.py:17
  671.8 13.0 %collective-permute-start.1 = (f32[2,32,768]{2,1,0:T(8,128)S(1)}, f32[2,32,768]{2,1,0:T(8,128)S(1)}, u32[]{:S(2)}, u32[]{:S(2)}) collective-permute-start(f32[2,32,768]{2,1,0:T(8,128)S(1)} %convolution_add_fusion.2), channel_id=1, source_target_pairs={{0,4},{4,8},{8,12},{12,16},{16,20},{20,24},{24,28},{28,32},{32,36}... | collective-permute-start | bytes 589832 | tf_op jit(solution)/shard_map/while/body/eval_jaxpr/ppermute | solution.py:17
  671.9 12.9 %collective-permute-start = (bf16[2,32,768]{2,1,0:T(8,128)(2,1)S(1)}, bf16[2,32,768]{2,1,0:T(8,128)(2,1)S(1)}, u32[]{:S(2)}, u32[]{:S(2)}) collective-permute-start(bf16[2,32,768]{2,1,0:T(8,128)(2,1)S(1)} %copy.19), channel_id=1, source_target_pairs={{0,4},{4,8},{8,12},{12,16},{16,20},{20,24},{24,28},{28,32},{32,36}... | collective-permute-start | bytes 294920 | tf_op jit(solution)/shard_map/while/body/eval_jaxpr/ppermute | solution.py:17
  688.6 12.1 %collective-permute-start.1 = (f32[2,32,768]{2,1,0:T(8,128)S(1)}, f32[2,32,768]{2,1,0:T(8,128)S(1)}, u32[]{:S(2)}, u32[]{:S(2)}) collective-permute-start(f32[2,32,768]{2,1,0:T(8,128)S(1)} %convolution_add_fusion.2), channel_id=1, source_target_pairs={{0,4},{4,8},{8,12},{12,16},{16,20},{20,24},{24,28},{28,32},{32,36}... | collective-permute-start | bytes 589832 | tf_op jit(solution)/shard_map/while/body/eval_jaxpr/ppermute | solution.py:17
  688.7 12.0 %collective-permute-start = (bf16[2,32,768]{2,1,0:T(8,128)(2,1)S(1)}, bf16[2,32,768]{2,1,0:T(8,128)(2,1)S(1)}, u32[]{:S(2)}, u32[]{:S(2)}) collective-permute-start(bf16[2,32,768]{2,1,0:T(8,128)(2,1)S(1)} %copy.19), channel_id=1, source_target_pairs={{0,4},{4,8},{8,12},{12,16},{16,20},{20,24},{24,28},{28,32},{32,36}... | collective-permute-start | bytes 294920 | tf_op jit(solution)/shard_map/while/body/eval_jaxpr/ppermute | solution.py:17
  858.0 12.4 %collective-permute-start.1 = (f32[2,32,768]{2,1,0:T(8,128)S(1)}, f32[2,32,768]{2,1,0:T(8,128)S(1)}, u32[]{:S(2)}, u32[]{:S(2)}) collective-permute-start(f32[2,32,768]{2,1,0:T(8,128)S(1)} %convolution_add_fusion.2), channel_id=1, source_target_pairs={{0,4},{4,8},{8,12},{12,16},{16,20},{20,24},{24,28},{28,32},{32,36}... | collective-permute-start | bytes 589832 | tf_op jit(solution)/shard_map/while/body/eval_jaxpr/ppermute | solution.py:17
  858.1 12.3 %collective-permute-start = (bf16[2,32,768]{2,1,0:T(8,128)(2,1)S(1)}, bf16[2,32,768]{2,1,0:T(8,128)(2,1)S(1)}, u32[]{:S(2)}, u32[]{:S(2)}) collective-permute-start(bf16[2,32,768]{2,1,0:T(8,128)(2,1)S(1)} %copy.19), channel_id=1, source_target_pairs={{0,4},{4,8},{8,12},{12,16},{16,20},{20,24},{24,28},{28,32},{32,36}... | collective-permute-start | bytes 294920 | tf_op jit(solution)/shard_map/while/body/eval_jaxpr/ppermute | solution.py:17
  874.2 12.9 %collective-permute-start.1 = (f32[2,32,768]{2,1,0:T(8,128)S(1)}, f32[2,32,768]{2,1,0:T(8,128)S(1)}, u32[]{:S(2)}, u32[]{:S(2)}) collective-permute-start(f32[2,32,768]{2,1,0:T(8,128)S(1)} %convolution_add_fusion.2), channel_id=1, source_target_pairs={{0,4},{4,8},{8,12},{12,16},{16,20},{20,24},{24,28},{28,32},{32,36}... | collective-permute-start | bytes 589832 | tf_op jit(solution)/shard_map/while/body/eval_jaxpr/ppermute | solution.py:17
  874.3 12.8 %collective-permute-start = (bf16[2,32,768]{2,1,0:T(8,128)(2,1)S(1)}, bf16[2,32,768]{2,1,0:T(8,128)(2,1)S(1)}, u32[]{:S(2)}, u32[]{:S(2)}) collective-permute-start(bf16[2,32,768]{2,1,0:T(8,128)(2,1)S(1)} %copy.19), channel_id=1, source_target_pairs={{0,4},{4,8},{8,12},{12,16},{16,20},{20,24},{24,28},{28,32},{32,36}... | collective-permute-start | bytes 294920 | tf_op jit(solution)/shard_map/while/body/eval_jaxpr/ppermute | solution.py:17
  890.8 12.0 %collective-permute-start.1 = (f32[2,32,768]{2,1,0:T(8,128)S(1)}, f32[2,32,768]{2,1,0:T(8,128)S(1)}, u32[]{:S(2)}, u32[]{:S(2)}) collective-permute-start(f32[2,32,768]{2,1,0:T(8,128)S(1)} %convolution_add_fusion.2), channel_id=1, source_target_pairs={{0,4},{4,8},{8,12},{12,16},{16,20},{20,24},{24,28},{28,32},{32,36}... | collective-permute-start | bytes 589832 | tf_op jit(solution)/shard_map/while/body/eval_jaxpr/ppermute | solution.py:17
  (113 other events, 1149.1 us)
Sparse Core Ops, SparseCore 0:
  12.9 60.5 all-reduce.4
  1008.1 96.1 reduce-scatter.1
where the time goes:
time: 1110 us
  waiting for transfers between devices  758 us (68%)
  local copies, waits for them, and re-layouts  130 us (12%)
  other arithmetic  117 us (11%)
  matrix products  52.2 us (5%)
  blocking collectives  23.1 us (2%)
  between operations  14.7 us (1%)
  starting transfers between devices  13 us (1%)
    ppermute x128, waiting for transfers between devices, from_behind(): lax.ppermute(array, axis, [(i, (i + by) % length) for i in range(length)])  626 us
    reduce_scatter x1, waiting for transfers between devices, shards(): lax.psum_scatter(image_grad.astype(jnp.bfloat16), 'narrow', scatter_dimen...  96.3 us
    dynamic_update_slice x64, other arithmetic, shift_turn(): lax.dynamic_update_slice_in_dim(grad_store, score_grad.reshape(1, text_ro...  46.9 us
    dynamic_update_slice x64, local copies, waits for them, and re-layouts, shift_turn(): lax.dynamic_update_slice_in_dim(text_store, moving_text.reshape(1, text_r...  41.2 us
    psum x1, waiting for transfers between devices, shards(): lax.psum(jnp.dot(hidden, w_down, preferred_element_type=jnp.float32), 'na...  35.3 us
    unnamed x1, blocking collectives  23.1 us
    dot_general x64, matrix products, pair_terms(): lax.dot_general(flat_text, images, (((1,), (1,)), ((), ())), preferred_el...  22.8 us
  transfers between devices with their start and end apart: 130, of which 66 were waited for; matrix products, arithmetic and copies ran while one was open for 4% of the time, Pallas kernels for 0%

commit v1 on v0

v1 whole, which is shorter than its diff:
```python
import functools
import math

import jax
import jax.numpy as jnp
from jax import lax
from jax.experimental import pallas as pl
from jax.experimental.pallas import tpu as pltpu
from jax.sharding import Mesh, PartitionSpec as P

D = 768
FACTOR = 1.75 / math.sqrt(768)
LN2 = math.log(2.0)
S2 = FACTOR / LN2


def lane_all(x, op):
    x = op(x, pltpu.roll(x, 64, 1))
    x = op(x, pltpu.roll(x, 32, 1))
    return x

def pair_block(s_ref, g_ref, r0, c0, gr0, len_row, lab_row, image_id):
    lane = lax.broadcasted_iota(jnp.int32, (8, 128), 1)
    tile = lax.broadcasted_iota(jnp.int32, (8, 128), 0)
    tok = tile * 4 + lane // 32
    valid = tok < len_row
    neg = jnp.where(valid, 0.0, -1e30).astype(jnp.float32)
    lenf = len_row.astype(jnp.float32)
    share = jnp.where(valid, 1.0 / lenf, 0.0)
    ss = []
    pm = None
    tms = []
    for k in range(8):
        s = s_ref[pl.ds(r0, 64), pl.ds(c0 + k * 128, 128)] * S2
        m = s + neg[k:k+1]
        pm = m if pm is None else jnp.maximum(pm, m)
        tms.append(jnp.max(s, axis=0, keepdims=True))
    pm = lane_all(pm, jnp.maximum)
    ps = None
    tss = []
    e1s, e2s = [], []
    for k in range(8):
        s = s_ref[pl.ds(r0, 64), pl.ds(c0 + k * 128, 128)] * S2
        e1 = jnp.exp2(s + neg[k:k+1] - pm)
        e2 = jnp.exp2(s - tms[k])
        ps = e1 if ps is None else ps + e1
        tss.append(jnp.sum(e2, axis=0, keepdims=True))
        e1s.append(e1); e2s.append(e2)
    ps = lane_all(ps, jnp.add)
    tm = jnp.concatenate(tms, axis=0)
    ts = jnp.concatenate(tss, axis=0)
    patch_pool = pm * LN2 + jnp.log(ps)
    token_pool = tm * LN2 + jnp.log(ts)
    a = jnp.sum(patch_pool, axis=0, keepdims=True) * (1.0 / 64)
    b = jnp.sum(token_pool * share, axis=0, keepdims=True)
    b = lane_all(b, jnp.add)
    logit = 4.0 * 0.5 * (a + b) - 26.0
    sign = jnp.where(lab_row == image_id, 1.0, -1.0).astype(jnp.float32)
    pg = -sign / (1.0 + jnp.exp(sign * logit))
    pg = pg * (2.0 * FACTOR)
    ca = (pg * (1.0 / 64)) / ps
    cb = pg * share / ts
    for k in range(8):
        g = e1s[k] * ca + e2s[k] * cb[k:k+1]
        g_ref[pl.ds(gr0, 64), pl.ds(c0 + k * 128, 128)] = g.astype(jnp.bfloat16)


def pair_kernel(img_ref, cap_ref, len_ref, lab_ref, base_ref, ig_ref, tg_ref, s_ref, g_ref):
    def chunk(q, _):
        r = pl.multiple_of(q * 256, 256)

        def sc(n, _):
            n0 = pl.multiple_of(n * 512, 512)
            s_ref[:, pl.ds(n0, 512)] = lax.dot_general(
                img_ref[pl.ds(r, 256), :], cap_ref[pl.ds(n0, 512), :], (((1,), (1,)), ((), ())),
                preferred_element_type=jnp.float32)
            return 0

        lax.fori_loop(0, 4, sc, 0)

        def el(b, _):
            i = b // 2
            r0 = pl.multiple_of(i * 64, 64)
            g0 = pl.multiple_of(r + r0, 64)
            grp = b % 2
            c0 = pl.multiple_of(grp * 1024, 1024)
            slot = q * 4 + i
            image_id = base_ref[0] + (slot // 2) * 8 + slot % 2
            pair_block(s_ref, g_ref, r0, c0, g0, len_ref[pl.ds(grp, 1), :], lab_ref[pl.ds(grp, 1), :], image_id)
            return 0

        lax.fori_loop(0, 8, el, 0)
        ig_ref[pl.ds(r, 256), :] = jnp.dot(
            g_ref[pl.ds(r, 256), :], cap_ref[...], preferred_element_type=jnp.float32)
        return 0

    lax.fori_loop(0, 4, chunk, 0)

    def tg(n, _):
        n0 = pl.multiple_of(n * 256, 256)
        tg_ref[pl.ds(n0, 256), :] = lax.dot_general(
            g_ref[:, pl.ds(n0, 256)], img_ref[...], (((0,), (0,)), ((), ())),
            preferred_element_type=jnp.float32)
        return 0

    lax.fori_loop(0, 8, tg, 0)


def pair_call(img, cap, ln, lab, base):
    return pl.pallas_call(
        pair_kernel,
        out_shape=(jax.ShapeDtypeStruct((1024, D), jnp.float32), jax.ShapeDtypeStruct((2048, D), jnp.float32)),
        in_specs=[pl.BlockSpec(memory_space=pltpu.VMEM)] * 4 + [pl.BlockSpec(memory_space=pltpu.SMEM)],
        out_specs=[pl.BlockSpec(memory_space=pltpu.VMEM)] * 2,
        scratch_shapes=[pltpu.VMEM((256, 2048), jnp.float32), pltpu.VMEM((1024, 2048), jnp.bfloat16)],
        compiler_params=pltpu.CompilerParams(vmem_limit_bytes=48 * 2**20),
    )(img, cap, ln, lab, base)


def layer_norm(mixed):
    center = mixed - jnp.mean(mixed, axis=-1, keepdims=True)
    spread = jnp.mean(center * center, axis=-1, keepdims=True)
    return center * lax.rsqrt(spread + 1e-6)


def shards(patches_in, w_up, w_down, captions, labels, lengths):
    capax = ("core", "xl", "y", "xh")
    n_i = lax.axis_index("xh") * 2 + lax.axis_index("core")
    cap_all = lax.all_gather(captions, capax, axis=0, tiled=True)
    meta = lax.all_gather(jnp.stack([labels, lengths], 1), capax, axis=0, tiled=True)
    cap_all = cap_all.reshape(2, 32, 32, D).transpose(0, 2, 1, 3).reshape(2048, D)
    lab = jnp.tile(meta[:, 0].reshape(2, 32), (1, 4))
    ln = jnp.tile(meta[:, 1].reshape(2, 32), (1, 4))
    flat_in = patches_in.reshape(512, D)
    hidden = jax.nn.gelu(jnp.dot(flat_in, w_up, preferred_element_type=jnp.float32)).astype(jnp.bfloat16)
    part = jnp.dot(hidden, w_down, preferred_element_type=jnp.float32)
    own = lax.psum_scatter(part, ("xh", "core"), scatter_dimension=0, tiled=True).astype(jnp.float32)
    own_in = lax.dynamic_slice_in_dim(flat_in, n_i * 128, 128, 0).astype(jnp.float32)
    image = layer_norm(own_in + own).astype(jnp.bfloat16)
    images = lax.all_gather(image, "z", axis=0, tiled=True)
    base = (((lax.axis_index("xl") * 4 + lax.axis_index("y")) * 8) * 8 + n_i * 2).astype(jnp.int32).reshape(1)
    ig, tg = pair_call(images, cap_all, ln, lab, base)
    ig = lax.psum_scatter(ig, "z", scatter_dimension=0, tiled=True).astype(jnp.float32)
    tg = tg.reshape(2, 32, 32, D).transpose(0, 2, 1, 3).reshape(2048, D)
    tg = lax.psum_scatter(tg, capax, scatter_dimension=0, tiled=True).astype(jnp.float32)
    return ig.reshape(2, 64, D), tg.reshape(2, 32, D)


def solution(mesh):
    grid = Mesh(mesh.devices.reshape(2, 4, 8, 2, 2), ("xl", "y", "z", "xh", "core"))
    wide = ("xl", "y", "z")
    narrow = ("xh", "core")
    both = wide + narrow
    return jax.shard_map(
        shards,
        mesh=grid,
        in_specs=(P(wide), P(None, narrow), P(narrow), P(both), P(both), P(both)),
        out_specs=(P(both), P(both)),
        check_vma=False,
    )
```

time: 1110 us -> 405 us (0.36)
  waiting for transfers between devices: 758 us -> 262 us
  other arithmetic: 117 us -> 4.13 us
  local copies, waits for them, and re-layouts: 130 us -> 19.3 us
  matrix products: 52.2 us -> 4.22 us
  blocking collectives: 23.1 us -> 64.8 us
  Pallas kernels: 0 us -> 33.6 us
  starting transfers between devices: 13 us -> 0.21 us
    ppermute x128 -> x0, waiting for transfers between devices: 626 us -> none  [from_behind(): lax.ppermute(array, axis, [(i, (i + by) % length) for i in range(length)])]
    reduce_scatter x1 -> x3, waiting for transfers between devices: 96.3 us -> 262 us  [the longest x1 185 us: shards(): lax.psum_scatter(tg, capax, scatter_dimension=0, tiled=True)]
    all_gather x0 -> x1, blocking collectives: none -> 64.8 us  [shards(): lax.all_gather(jnp.stack([labels, lengths], 1), capax, axis=0, tiled=True)]
    dot_general x130 -> x1, matrix products: 52.2 us -> 4.22 us  [shards(): part = jnp.dot(hidden, w_down, preferred_element_type=jnp.float32)]
    dynamic_update_slice x64 -> x0, other arithmetic: 46.9 us -> none  [shift_turn(): lax.dynamic_update_slice_in_dim(grad_store, score_grad.reshape(1, text_ro...]
    dynamic_update_slice x64 -> x0, local copies, waits for them, and re-layouts: 41.2 us -> none  [shift_turn(): lax.dynamic_update_slice_in_dim(text_store, moving_text.reshape(1, text_r...]
    psum x1 -> x0, waiting for transfers between devices: 35.3 us -> none  [shards(): lax.psum(jnp.dot(hidden, w_down, preferred_element_type=jnp.float32), 'na...]
    pallas_call x0 -> x1, Pallas kernels: none -> 33.6 us  [pair_call(): pl.pallas_call(pair_kernel, out_shape=(jax.ShapeDtypeStruct((1024, D), jn...]
  transfers between devices with their start and end apart: 130 -> 5, of which waited for: 66 -> 3; matrix products, arithmetic and copies ran while one was open for 4% -> 5% of each run, Pallas kernels for 0% -> 0%
where the time goes in v1:
time: 405 us; the launch traced here: 404 us
  waiting for transfers between devices  262 us (65%)
  blocking collectives  64.8 us (16%)
  Pallas kernels  33.6 us (8%)
  local copies, waits for them, and re-layouts  19.3 us (5%)
  between operations  15.7 us (4%)
  matrix products  4.22 us (1%)
  other arithmetic  4.13 us (1%)
    reduce_scatter x1, waiting for transfers between devices, shards(): lax.psum_scatter(tg, capax, scatter_dimension=0, tiled=True)  185 us
    all_gather x1, blocking collectives, shards(): lax.all_gather(jnp.stack([labels, lengths], 1), capax, axis=0, tiled=True)  64.8 us
    reduce_scatter x1, waiting for transfers between devices, shards(): lax.psum_scatter(part, ('xh', 'core'), scatter_dimension=0, tiled=True)  43.9 us
    pallas_call x1, Pallas kernels, pair_call(): pl.pallas_call(pair_kernel, out_shape=(jax.ShapeDtypeStruct((1024, D), jn...  33.6 us
    reduce_scatter x1, waiting for transfers between devices, shards(): lax.psum_scatter(ig, 'z', scatter_dimension=0, tiled=True)  33 us
    reshape x1, local copies, waits for them, and re-layouts, shards(): tg = tg.reshape(2, 32, 32, D).transpose(0, 2, 1, 3).reshape(2048, D)  9.09 us
  transfers between devices with their start and end apart: 5, of which 3 were waited for; matrix products, arithmetic and copies ran while one was open for 5% of the time, Pallas kernels for 0%

profile of v1, /device:TPU:1, one launch (start us, length us, event | category | flops | bytes accessed | tf_op | source)
XLA Modules:
  0.0 404.3 jit_solution(10731302254307959874)
XLA Ops:
  8.1 1.2 copy-done
  9.3 4.2 %fusion.8 = f32[512,768]{1,0:T(8,128)} fusion(bf16[768,768]{1,0:T(8,128)(2,1)S(1)} %copy-done, bf16[512,768]{1,0:T(8,128)(2,1)} %bitcast.23, bf16[768,768]{1,0:T(8,128)(2,1)} %param.7), kind=kOutput, calls=%fused_computation.9 | convolution fusion | flops 1211498496 | bytes 4718592 | tf_op jit(solution)/shard_map/dot_general | solution.py:136
  13.5 0.0 all-gather.6.cloned.1.call-start
  13.6 0.5 all-gather.6.cloned.1.call-update
  14.2 43.9 %reduce-scatter.4.cloned.1.call-done = f32[128,768]{1,0:T(8,128)} async-done(((f32[512,768]{1,0:T(8,128)}), f32[128,768]{1,0:T(8,128)}) %reduce-scatter.4.cloned.1.call-update) | async-done | bytes 393232 | tf_op jit(solution)/shard_map/reduce_scatter | solution.py:137
  58.0 1.1 fusion.14
  59.2 1.2 multiply_reduce_fusion
  60.4 1.8 multiply_convert_fusion
  62.2 0.0 reduce-scatter.6.cloned.1.call-start
  62.3 0.1 copy.16
  62.4 64.8 %all-gather = s32[32,2,2]{2,1,0:T(2,128)S(1)} all-gather(s32[1,2,2]{2,1,0:T(2,128)S(1)} %bitcast.28), channel_id=1, replica_groups=mesh['xl'=2,'y'=4,'z'=8,'xh'=2,'core'=2] {'core','xl','y','xh'}, dimensions={0}, use_global_device_ids=true | all-gather | bytes 528 | tf_op jit(solution)/shard_map/all_gather | solution.py:130
  127.2 0.2 slice_reduce_fusion
  127.3 0.1 tile.20
  127.4 0.1 tile.22.len_ref
  127.5 0.1 tile.23
  127.6 0.1 tile.25.lab_ref
  127.7 5.3 %copy.15 = bf16[2,32,32,768]{3,1,2,0:T(8,128)(2,1)} copy(bf16[2,32,32,768]{3,2,1,0:T(8,128)(2,1)} %bitcast.22) | data formatting | bytes 6291456 | tf_op jit(solution)/shard_map/reshape | solution.py:131
  133.0 1.4 copy-done.2
  134.4 33.6 %shard_map.77 = (f32[1024,768]{1,0:T(8,128)S(1)}, f32[2048,768]{1,0:T(8,128)}) custom-call(bf16[1024,768]{1,0:T(8,128)(2,1)S(1)} %copy-done.2, bf16[2048,768]{1,0:T(8,128)(2,1)} %bitcast.20, s32[2,128]{1,0:T(2,128)S(1)} %tile.22.len_ref, s32[2,128]{1,0:T(2,128)S(1)} %tile.25.lab_ref, s32[1]{0:T(128)} %bitcast.8.base_ref), custom_call_target="tpu_custom_call" | custom-call | tf_op jit(solution)/shard_map/pallas_call | solution.py:110
  168.0 1.7 copy-done.1
  169.7 0.0 reduce-scatter.8.cloned.1.call-start
  169.7 9.1 %copy.18 = f32[2,32,32,768]{3,1,2,0:T(8,128)} copy(f32[2,32,32,768]{3,2,1,0:T(8,128)} %bitcast.21) | data formatting | bytes 12582912 | tf_op jit(solution)/shard_map/reshape | solution.py:144
  178.9 33.0 %reduce-scatter.6.cloned.1.call-done = f32[128,768]{1,0:T(8,128)} async-done(((f32[1024,768]{1,0:T(8,128)}), f32[128,768]{1,0:T(8,128)}) %reduce-scatter.6.cloned.1.call-update) | async-done | bytes 393232 | tf_op jit(solution)/shard_map/reduce_scatter | solution.py:143
  211.8 184.8 %reduce-scatter.8.cloned.1.call-done = f32[64,768]{1,0:T(8,128)} async-done(((f32[2048,768]{1,0:T(8,128)}), f32[64,768]{1,0:T(8,128)}) %reduce-scatter.8.cloned.1.call-update) | async-done | bytes 196624 | tf_op jit(solution)/shard_map/reduce_scatter | solution.py:145
  (22 shorter events, 0.2 us)
Async XLA Ops:
  8.0 1.3 copy-start
  8.0 50.0 %reduce-scatter.4.cloned.1.call-start = ((), (), s32[]{:S(2)}) async-start(), calls=%async_computation.3 | async-start | bytes 1966080 | tf_op jit(solution)/shard_map/reduce_scatter | solution.py:137
  13.5 44.6 %copy-start.3 = (bf16[8,64,768]{2,1,0:T(8,128)(2,1)S(1)}, bf16[8,64,768]{2,1,0:T(8,128)(2,1)}, u32[]{:S(2)}) copy-start(bf16[8,64,768]{2,1,0:T(8,128)(2,1)} %param.6) | copy-start | bytes 2359300
  13.5 48.8 %copy-start.4 = (s32[2]{0:T(128)S(1)}, s32[2]{0:T(128)}, u32[]{:S(2)}) copy-start(s32[2]{0:T(128)} %param.11) | copy-start | bytes 28
  13.5 48.8 %copy-start.5 = (s32[2]{0:T(128)S(1)}, s32[2]{0:T(128)}, u32[]{:S(2)}) copy-start(s32[2]{0:T(128)} %param.10) | copy-start | bytes 28
  13.5 114.2 %all-gather.6.cloned.1.call-start = ((), (), s32[]{:S(2)}) async-start(), calls=%async_computation.5 | async-start | bytes 3244032 | tf_op jit(solution)/shard_map/all_gather | solution.py:129
  14.1 118.9 %all-gather.4.cloned.1.call-start = ((), (), s32[]{:S(2)}) async-start(), calls=%async_computation.4 | async-start | bytes 1769472 | tf_op jit(solution)/shard_map/all_gather | solution.py:140
  62.2 149.6 %reduce-scatter.6.cloned.1.call-start = ((), (), s32[]{:S(2)}) async-start(), calls=%async_computation.6 | async-start | bytes 3538944 | tf_op jit(solution)/shard_map/reduce_scatter | solution.py:143
  133.0 1.4 copy-start.2
  168.0 1.7 copy-start.1
  169.7 227.0 %reduce-scatter.8.cloned.1.call-start = ((), (), s32[]{:S(2)}) async-start(), calls=%async_computation.7 | async-start | bytes 6488064 | tf_op jit(solution)/shard_map/reduce_scatter | solution.py:145
Sparse Core Ops, SparseCore 0:
  13.6 44.3 reduce-scatter.3
Sparse Core Ops, SparseCore 1:
  15.8 73.7 all-gather.5
  91.9 34.8 all-gather.3
  169.8 42.0 reduce-scatter.5
  215.1 181.5 reduce-scatter.7
